TPU v7x, 512 devices: a whole 4x4x16 slice. The times are simulated.
512 devices in a mesh: img: 64 (over x, y, z_lo), bas: 8 (over z_hi, core).
Axes of the slice: x: 4, y: 4, z: 16 (z_hi: 4, z_lo: 4; z = z_hi * 4 + z_lo), core: 2. Of those that a mesh axis runs over, the one named last changes fastest.
Arguments:
- polar_images: bfloat16 [2048, 64, 512], P('img', 'bas'), may hold values from -6 to 6
- ctf_groups: int32 [2048], P('img'), may hold values from 0 to 63
- ctf_table: float32 [64, 64], replicated, may hold values from -1 to 1
- radial_basis: bfloat16 [256, 64, 64], P('bas'), may hold values from -0.75 to 0.75
- order_counts: int32 [256], P('bas'), may hold values from 1 to 64, as said below
Outputs:
- covariance: float32 [64, 16384], P('img', 'bas')
Inputs may be any that keep to these rules, and one draw needn't show every extreme that they name: `order_counts`: order 0 has 64 basis functions; every other order q has max(1, 64 - (q * 64) // 256 - j) of them, where j is one of 0, 1, 2, 3 and may differ from order to order.
All inputs are finite; a program needn't handle non-finite values.
Results may differ from a plain program's by a relative error of at most 0.0015.
Values may be sent and summed in bfloat16 or wider, within the bound.
No kernel may reach another device: no remote copies, remote signals or barrier semaphores. Data moves between devices by JAX's collectives and lax.ppermute only.
A program may use at most 64 MiB of HBM per device.

v0:
```python
import math

import jax
import jax.numpy as jnp
from jax import lax
from jax.sharding import PartitionSpec as P


def angular_table(orders, angles):
    steps = jnp.arange(angles, dtype=jnp.int32)
    phase = steps[:, None] * orders[None, :] % angles
    theta = phase.astype(jnp.float32) * (2.0 * math.pi / angles)
    table = jnp.stack([jnp.cos(theta), jnp.sin(theta)], axis=-1) * (1.0 / math.sqrt(angles))
    return table.reshape(angles, -1).astype(jnp.bfloat16)


def local(polar_images, ctf_groups, ctf_table, radial_basis, order_counts):
    images_dev, radii_dev, angles = polar_images.shape
    orders_dev, radii, kmax = radial_basis.shape
    img_size = lax.axis_size("img")
    classes = ctf_table.shape[0]
    onehot = (ctf_groups[:, None] == jnp.arange(classes, dtype=jnp.int32)[None, :]).astype(
        jnp.float32
    )
    weights = jnp.dot(onehot, ctf_table, precision=lax.Precision.HIGHEST)
    kept = (jnp.arange(kmax, dtype=jnp.int32)[None, :] < order_counts[:, None]).astype(jnp.float32)
    whole = lax.all_gather(polar_images, "bas", axis=1, tiled=True)
    orders = lax.axis_index("bas") * orders_dev + jnp.arange(orders_dev, dtype=jnp.int32)
    table = angular_table(orders, angles)
    weighted = (whole.astype(jnp.float32) * weights[:, :, None]).astype(jnp.bfloat16)
    spectra = jnp.dot(weighted.reshape(-1, angles), table, preferred_element_type=jnp.float32)
    spectra = spectra.astype(jnp.bfloat16).reshape(images_dev, radii, 2 * orders_dev)
    shaped = spectra.reshape(spectra.shape[0], radii, orders_dev, 2)
    coeffs = jnp.einsum("brqc,qrk->bqck", shaped, radial_basis, preferred_element_type=jnp.float32)
    coeffs = (coeffs * kept[None, :, None, :]).astype(jnp.bfloat16)
    rows = kmax // img_size
    scale = 1.0 / (images_dev * img_size)
    full = jnp.einsum("bqck,bqcl->kql", coeffs, coeffs, preferred_element_type=jnp.float32)
    total = lax.psum(full.reshape(kmax, orders_dev * kmax), "img")
    gram = lax.dynamic_slice_in_dim(total, lax.axis_index("img") * rows, rows, 0)
    return gram * scale


def solution(mesh):
    placed = (P("img", "bas", None), P("img"), P(), P("bas", None, None), P("bas"))
    return jax.shard_map(
        local, mesh=mesh, in_specs=placed, out_specs=P("img", "bas"), check_vma=False
    )
```

profile of v0, /device:TPU:128, one launch (start us, length us, event | category | flops | bytes accessed | tf_op | source)
XLA Modules:
  0.0 802.6 jit_solution(7129516911920482153)
XLA Ops:
  6.5 0.0 copy-start
  6.5 0.0 all-gather.2.cloned.1.call-start
  6.5 0.7 all-gather.2.cloned.1.call-update
  7.3 0.0 all-reduce.2.cloned.1.call-start
  7.3 0.3 fusion.14
  7.7 0.1 copy.8
  7.8 0.7 fusion.16
  8.5 1.0 fusion.15
  9.5 61.4 %all-gather.2.cloned.1.call-done = bf16[32,64,512]{2,1,0:T(8,128)(2,1)} async-done(((bf16[32,8,512]{2,1,0:T(8,128)(2,1)}), bf16[32,64,512]{2,1,0:T(8,128)(2,1)}) %all-gather.2.cloned.1.call-update) | async-done | bytes 2097168 | tf_op jit(solution)/shard_map/all_gather | solution.py:27
  70.9 2.1 multiply_convert_fusion
  73.0 0.8 convolution_convert_fusion
  73.7 0.5 reshape_reshape.3
  74.2 0.0 copy-done
  74.2 0.6 fusion.2
  74.8 1.1 copy.9
  75.9 0.0 all-reduce.2.cloned.1.call-update
  76.0 718.4 %all-reduce.2.cloned.1.call-done = f32[64,2048]{1,0:T(8,128)} async-done(((f32[64,2048]{1,0:T(8,128)}), f32[64,2048]{1,0:T(8,128)}) %all-reduce.2.cloned.1.call-update) | async-done | bytes 524304 | tf_op jit(solution)/shard_map/psum | solution.py:39
  794.4 1.4 dynamic-slice_multiply_fusion
  (3 shorter events, 0.1 us)
Async XLA Ops:
  6.5 67.7 %copy-start = (bf16[32,64,64]{2,1,0:T(8,128)(2,1)S(1)}, bf16[32,64,64]{2,1,0:T(8,128)(2,1)}, u32[]{:S(2)}) copy-start(bf16[32,64,64]{2,1,0:T(8,128)(2,1)} %param.8) | copy-start | bytes 786436
  6.5 64.3 %all-gather.2.cloned.1.call-start = ((), (), s32[]{:S(2)}) async-start(), calls=%async_computation | async-start | bytes 2359296 | tf_op jit(solution)/shard_map/all_gather | solution.py:27
  7.3 787.1 %all-reduce.2.cloned.1.call-start = ((), (), s32[]{:S(2)}) async-start(), calls=%async_computation.1 | async-start | bytes 1048576 | tf_op jit(solution)/shard_map/psum | solution.py:39
Sparse Core Ops, SparseCore 0:
  9.5 61.3 all-gather.1
  76.1 718.2 all-reduce.1
where the time goes:
time: 803 us
  waiting for transfers between devices  781 us (97%)
  between operations  13.5 us (2%)
    psum x1, waiting for transfers between devices, local(): total = lax.psum(full.reshape(kmax, orders_dev * kmax), 'img')  718 us
    all_gather x1, waiting for transfers between devices, local(): whole = lax.all_gather(polar_images, 'bas', axis=1, tiled=True)  61.4 us
  transfers between devices with their start and end apart: 2, of which 2 were waited for; matrix products, arithmetic and copies ran while one was open for 0% of the time, Pallas kernels for 0%

commit v1 on v0

v1 whole, which is shorter than its diff:
```python
import math

import jax
import jax.numpy as jnp
from jax import lax
from jax.sharding import PartitionSpec as P


def angular_table(orders, angles):
    steps = jnp.arange(angles, dtype=jnp.int32)
    phase = steps[:, None] * orders[None, :] % angles
    theta = phase.astype(jnp.float32) * (2.0 * math.pi / angles)
    table = jnp.stack([jnp.cos(theta), jnp.sin(theta)], axis=-1) * (1.0 / math.sqrt(angles))
    return table.reshape(angles, -1).astype(jnp.bfloat16)


def local(polar_images, ctf_groups, ctf_table, radial_basis, order_counts):
    images_dev, radii_dev, angles = polar_images.shape
    orders_dev, radii, kmax = radial_basis.shape
    img_size, bas_size = lax.axis_size("img"), lax.axis_size("bas")
    classes = ctf_table.shape[0]
    onehot = (ctf_groups[:, None] == jnp.arange(classes, dtype=jnp.int32)[None, :]).astype(
        jnp.float32
    )
    own = lax.dynamic_slice_in_dim(ctf_table, lax.axis_index("bas") * radii_dev, radii_dev, 1)
    weights = jnp.dot(onehot, own, precision=lax.Precision.HIGHEST)
    kept = (jnp.arange(kmax, dtype=jnp.int32)[None, :] < order_counts[:, None]).astype(jnp.float32)
    table = angular_table(jnp.arange(orders_dev * bas_size, dtype=jnp.int32), angles)
    weighted = (polar_images.astype(jnp.float32) * weights[:, :, None]).astype(jnp.bfloat16)
    spectra = jnp.einsum(
        "nt,tm->mn", weighted.reshape(-1, angles), table, preferred_element_type=jnp.float32
    ).astype(jnp.bfloat16)
    parts = spectra.reshape(bas_size, 2 * orders_dev, images_dev * radii_dev)
    parts = lax.all_to_all(parts, "bas", 0, 0, tiled=True)
    shaped = parts.reshape(bas_size, orders_dev, 2, images_dev, radii_dev)
    basis = radial_basis.reshape(orders_dev, bas_size, radii_dev, kmax)
    coeffs = jnp.einsum("sqcbr,qsrk->bqck", shaped, basis, preferred_element_type=jnp.float32)
    coeffs = (coeffs * kept[None, :, None, :]).astype(jnp.bfloat16)
    scale = 1.0 / (images_dev * img_size)
    full = jnp.einsum("bqck,bqcl->kql", coeffs, coeffs, preferred_element_type=jnp.float32)
    rows = kmax // img_size
    sent = full.astype(jnp.bfloat16).reshape(img_size, rows * orders_dev * kmax // 128, 128)
    got = lax.all_to_all(sent, "img", 0, 0, tiled=True)
    gram = jnp.sum(got.astype(jnp.float32), axis=0)
    return gram.reshape(rows, orders_dev * kmax) * scale


def solution(mesh):
    placed = (P("img", "bas", None), P("img"), P(), P("bas", None, None), P("bas"))
    return jax.shard_map(
        local, mesh=mesh, in_specs=placed, out_specs=P("img", "bas"), check_vma=False
    )
```

time: 803 us -> 72.1 us (0.09)
  the two profiles are of different devices: /device:TPU:128 before, /device:TPU:6 now
where the time goes in v1:
time: 72.1 us; the launch traced here: 70.9 us
  blocking collectives  21.8 us (30%)
  waiting for transfers between devices  19.1 us (26%)
  starting transfers between devices  15.1 us (21%)
  local copies, waits for them, and re-layouts  6.88 us (10%)
  matrix products  5 us (7%)
  other arithmetic  2.9 us (4%)
    all_to_all x1, blocking collectives, local(): got = lax.all_to_all(sent, 'img', 0, 0, tiled=True)  21.8 us
    all_to_all x1, waiting for transfers between devices, local(): parts = lax.all_to_all(parts, 'bas', 0, 0, tiled=True)  19.1 us
    all_to_all x1, starting transfers between devices, local(): parts = lax.all_to_all(parts, 'bas', 0, 0, tiled=True)  15.1 us
    reshape x1, local copies, waits for them, and re-layouts, local(): shaped = parts.reshape(bas_size, orders_dev, 2, images_dev, radii_dev)  5.87 us
    dot_general x1, matrix products, local(): jnp.einsum('sqcbr,qsrk->bqck', shaped, basis, preferred_element_type=jnp....  3.34 us
    sin x1, other arithmetic, angular_table(): jnp.sin(theta)  2.06 us
  transfers between devices with their start and end apart: 1, of which 1 were waited for; matrix products, arithmetic and copies ran while one was open for 0% of the time, Pallas kernels for 0%

profile of v1, /device:TPU:6, one launch (start us, length us, event | category | flops | bytes accessed | tf_op | source)
XLA Modules:
  0.0 70.9 jit_solution(7081530603239999162)
XLA Ops:
  0.0 0.0 copy-start
  0.0 0.0 copy-start.2
  0.0 0.0 copy-start.1
  0.0 2.1 %fusion.18 = (f32[512,256,1]{1,0,2:T(8,128)S(1)}, f32[512,256,1]{1,0,2:T(8,128)S(1)}) fusion(), kind=kLoop, calls=%fused_computation.25 | loop fusion | flops 1835008 | bytes 1048576 | tf_op jit(solution)/shard_map/sin | solution.py:13
  2.1 0.1 fusion.3
  2.2 0.5 copy.14
  2.7 0.2 convert_element_type.62
  2.9 0.0 copy-done.4
  2.9 0.0 copy-done.3
  3.0 0.2 fusion.20
  3.1 0.0 copy-done.2
  3.2 1.1 %convolution_convert_fusion = bf16[512,256]{1,0:T(8,128)(2,1)} fusion(bf16[512,512]{0,1:T(8,128)(2,1)S(1)} %convert_element_type.62, bf16[32,8,512]{2,1,0:T(8,128)(2,1)S(1)} %copy-done.2, f32[32,8]{1,0:T(8,128)S(1)} %fusion.20), kind=kOutput, calls=%fused_computation.4 | convolution fusion | flops 134742016 | bytes 1049600 | tf_op jit(solution)/shard_map/nt,tm->mn/dot_general | solution.py:30
  4.3 15.1 %all-to-all-start = ((bf16[8,64,256]{2,1,0:T(8,128)(2,1)}), bf16[8,64,256]{2,1,0:T(8,128)(2,1)S(1)}, u32[]{:S(2)}, u32[]{:S(2)}) async-start(bf16[8,64,256]{2,1,0:T(8,128)(2,1)} %bitcast.1), calls=%async_computation | async-start | bytes 524288 | tf_op jit(solution)/shard_map/all_to_all | solution.py:34
  19.4 0.0 copy-done.1
  19.4 0.1 fusion.22
  19.4 19.1 %all-to-all-done = bf16[8,64,256]{2,1,0:T(8,128)(2,1)S(1)} async-done(((bf16[8,64,256]{2,1,0:T(8,128)(2,1)}), bf16[8,64,256]{2,1,0:T(8,128)(2,1)S(1)}, u32[]{:S(2)}, u32[]{:S(2)}) %all-to-all-start) | async-done | bytes 262176 | tf_op jit(solution)/shard_map/all_to_all | solution.py:34
  38.5 5.9 %reshape.130 = bf16[8,32,2,32,8]{4,3,2,1,0:T(8,128)(2,1)} reshape(bf16[8,64,256]{2,1,0:T(8,128)(2,1)S(1)} %all-to-all-done) | data formatting | bytes 524288 | tf_op jit(solution)/shard_map/reshape | solution.py:35
  44.4 0.0 copy-done
  44.4 3.3 %fusion = f32[32,2,32,64,1]{3,2,0,1,4:T(8,128)S(1)} fusion(bf16[8,32,2,32,8]{4,3,2,1,0:T(8,128)(2,1)} %reshape.130, bf16[32,64,64]{2,1,0:T(8,128)(2,1)S(1)} %copy-done), kind=kOutput, calls=%fused_computation | convolution fusion | flops 16777216 | bytes 1048576 | tf_op jit(solution)/shard_map/sqcbr,qsrk->bqck/dot_general | solution.py:37
  47.8 0.4 fusion.2
  48.1 0.3 copy.20
  48.4 21.8 %all_to_all.10 = bf16[64,16,128]{2,1,0:T(8,128)(2,1)S(1)} all-to-all(bf16[64,16,128]{2,1,0:T(8,128)(2,1)S(1)} %copy.20), channel_id=1, replica_groups=mesh['img'=64,'bas'=8] {'img'}, dimensions={0} | all-to-all | bytes 524288 | tf_op jit(solution)/shard_map/all_to_all | solution.py:43
  70.2 0.1 convert_reduce_fusion
  70.3 0.6 broadcast_multiply_fusion
  (2 shorter events, 0.0 us)
Async XLA Ops:
  0.0 44.4 %copy-start = (bf16[32,64,64]{2,1,0:T(8,128)(2,1)S(1)}, bf16[32,64,64]{2,1,0:T(8,128)(2,1)}, u32[]{:S(2)}) copy-start(bf16[32,64,64]{2,1,0:T(8,128)(2,1)} %param.8) | copy-start | bytes 786436
  0.0 2.9 %copy-start.4 = (s32[32]{0:T(128)S(1)}, s32[32]{0:T(128)}, u32[]{:S(2)}) copy-start(s32[32]{0:T(128)} %param.6) | copy-start | bytes 388
  0.0 2.9 %copy-start.3 = (f32[64,64]{1,0:T(8,128)S(1)}, f32[64,64]{1,0:T(8,128)}, u32[]{:S(2)}) copy-start(f32[64,64]{1,0:T(8,128)} %param.7) | copy-start | bytes 49156
  0.0 3.1 %copy-start.2 = (bf16[32,8,512]{2,1,0:T(8,128)(2,1)S(1)}, bf16[32,8,512]{2,1,0:T(8,128)(2,1)}, u32[]{:S(2)}) copy-start(bf16[32,8,512]{2,1,0:T(8,128)(2,1)} %param.5) | copy-start | bytes 786436
  0.0 19.3 %copy-start.1 = (s32[32]{0:T(128)S(1)}, s32[32]{0:T(128)}, u32[]{:S(2)}) copy-start(s32[32]{0:T(128)} %param.9) | copy-start | bytes 388
  4.3 34.3 %all-to-all-start = ((bf16[8,64,256]{2,1,0:T(8,128)(2,1)}), bf16[8,64,256]{2,1,0:T(8,128)(2,1)S(1)}, u32[]{:S(2)}, u32[]{:S(2)}) async-start(bf16[8,64,256]{2,1,0:T(8,128)(2,1)} %bitcast.1), calls=%async_computation | async-start | bytes 524288 | tf_op jit(solution)/shard_map/all_to_all | solution.py:34

commit v2 on v0

v2 whole, which is shorter than its diff:
```python
import functools
import functools
import math

import jax
import jax.numpy as jnp
import ml_dtypes
import numpy as np
from jax import lax
from jax.experimental import pallas as pl
from jax.experimental.pallas import tpu as pltpu
from jax.sharding import PartitionSpec as P

F32, BF16 = jnp.float32, jnp.bfloat16
NT = (((1,), (1,)), ((), ()))


def angular_table(orders, angles):
    phase = np.arange(angles)[:, None] * np.arange(orders)[None, :] % angles
    theta = phase.astype(np.float32) * np.float32(2.0 * math.pi / angles)
    table = np.stack([np.cos(theta), np.sin(theta)], axis=-1) * np.float32(1.0 / math.sqrt(angles))
    table = table.reshape(angles // 8, 8, 2, orders).transpose(2, 0, 1, 3)
    return table.astype(ml_dtypes.bfloat16)


def transform(first_of, groups_in, ctf_in, images_in, table_in, parts_out, *scratch):
    groups, ctf, images, table, weighted, parts, sem_in, sem_out = scratch
    size, rows, lanes = parts.shape
    classes, radii = ctf.shape
    radii_dev = radii // size
    width = lanes // 2
    halves = table.shape[0]
    copies = [
        pltpu.make_async_copy(source, target, sem_in.at[n])
        for n, (source, target) in enumerate(
            [(groups_in, groups), (ctf_in, ctf), (images_in, images)]
            + [(table_in.at[n], table.at[n]) for n in range(halves)]
        )
    ]
    for copy in copies:
        copy.start()
    first = lax.axis_index("bas") * radii_dev
    shape = (radii_dev, radii)
    own = lax.broadcasted_iota(jnp.int32, shape, 1) == first + lax.broadcasted_iota(jnp.int32, shape, 0)
    copies[0].wait()
    copies[1].wait()

    def weight(i):
        row = ctf[pl.ds(groups[i], 1), :]
        return jnp.sum(jnp.where(own, row, 0.0), axis=1, keepdims=True)

    step = 16 // radii_dev
    scales = [
        jnp.concatenate([weight(i + j) for j in range(step)], axis=0)
        for i in range(0, groups.shape[0], step)
    ]
    copies[2].wait()
    for n, scale in enumerate(scales):
        block = slice(n * 16, (n + 1) * 16)
        weighted[block, :] = (images[block, :].astype(F32) * scale).astype(BF16)
    low = lax.broadcasted_iota(jnp.int32, (rows, lanes), 1) < width
    sends = []
    for half in range(halves):
        copies[3 + half].wait()
        columns = table[half].reshape(weighted.shape[1], -1)
        spectra = jnp.dot(weighted[...], columns, preferred_element_type=F32)
        for pair in range(columns.shape[1] // lanes):
            block = spectra[:, pair * lanes : (pair + 1) * lanes]
            one, two = block[:rows], block[rows:]
            turned_one, turned_two = pltpu.roll(one, width, 1), pltpu.roll(two, width, 1)
            for n, value in enumerate((jnp.where(low, one, turned_two), jnp.where(low, turned_one, two))):
                order = half * (size // halves) + 2 * pair + n
                place = (order - first_of) % size
                parts[place] = value.astype(BF16)
                send = pltpu.make_async_copy(parts.at[place], parts_out.at[place], sem_out.at[place])
                send.start()
                sends.append(send)
    for send in sends:
        send.wait()


def covariances(first_of, last_of, parts_ref, basis, out, by_order, staged):
    sources, rows, lanes = parts_ref.shape
    pairs, wide, radii = basis.shape
    radii_dev = radii // sources
    lows = rows // radii_dev
    width = lanes // 2
    half = wide // 2
    step = 16 // radii_dev
    for i in range(0, lows, step):
        block = parts_ref[:, i * radii_dev : (i + step) * radii_dev, :].astype(F32)
        for j in range(step):
            one = block[:, j * radii_dev : (j + 1) * radii_dev, :]
            one = jnp.concatenate([one[(n - first_of) % sources] for n in range(sources)], axis=0)
            by_order[(i + j) * lanes : (i + j + 1) * lanes, :] = one.T
    same = (lax.broadcasted_iota(jnp.int32, (wide, wide), 0) < half) == (
        lax.broadcasted_iota(jnp.int32, (wide, wide), 1) < half
    )
    for pair in range(pairs):
        rows_of = [
            by_order[pl.ds(high * width + 4 * pair + 2 * order + c, lows, stride=lanes), :]
            for order in range(2)
            for high in range(2)
            for c in range(2)
        ]
        spectra = jnp.concatenate(rows_of, axis=0).astype(BF16)
        coeffs = lax.dot_general(basis[pair], spectra, NT, preferred_element_type=F32)
        coeffs = jnp.where(same, coeffs, 0.0).astype(BF16)
        gram = lax.dot_general(coeffs, coeffs, NT, preferred_element_type=F32)
        staged[pl.ds(pair, half, stride=pairs), :] = gram[:half] + gram[half:]
    grams = staged[...].astype(BF16).reshape(out.shape)
    out[...] = grams
    if last_of:
        chunk = out.shape[0] // last_of[1]
        for here, there in ((0, last_of[0]), (last_of[0], 0)):
            out[here * chunk : (here + 1) * chunk] = grams[there * chunk : (there + 1) * chunk]


def local(table, polar_images, ctf_groups, ctf_table, radial_basis, order_counts):
    images_dev, radii_dev, angles = polar_images.shape
    orders_dev, radii, kmax = radial_basis.shape
    img_size, bas_size = lax.axis_size("img"), lax.axis_size("bas")
    hbm = pl.BlockSpec(memory_space=pltpu.HBM)
    vmem = pl.BlockSpec(memory_space=pltpu.VMEM)
    lows = images_dev // 2
    lanes = 4 * orders_dev
    shape = (bas_size, lows * radii_dev, lanes)
    first_of = bas_size // 2
    bas_order = [(n + first_of) % bas_size for n in range(bas_size)]
    images = polar_images.reshape(-1, angles)
    parts = pl.pallas_call(
        functools.partial(transform, first_of),
        out_shape=jax.ShapeDtypeStruct(shape, BF16),
        in_specs=[hbm] * 4,
        out_specs=hbm,
        scratch_shapes=[
            pltpu.SMEM(ctf_groups.shape, jnp.int32),
            pltpu.VMEM(ctf_table.shape, F32),
            pltpu.VMEM(images.shape, BF16),
            pltpu.VMEM(table.shape, BF16),
            pltpu.VMEM(images.shape, BF16),
            pltpu.VMEM(shape, BF16),
            pltpu.SemaphoreType.DMA((3 + table.shape[0],)),
            pltpu.SemaphoreType.DMA((bas_size,)),
        ],
        compiler_params=pltpu.CompilerParams(vmem_limit_bytes=60 * 2**20),
        name="transform",
    )(ctf_groups, ctf_table, images, table)
    parts, radial_basis, order_counts = lax.optimization_barrier((parts, radial_basis, order_counts))
    parts = lax.all_to_all(parts, "bas", 0, 0, tiled=True, axis_index_groups=[bas_order])
    kept = jnp.arange(kmax, dtype=jnp.int32)[None, :] < order_counts[:, None]
    basis = jnp.where(kept[:, None, :], radial_basis, jnp.zeros((), BF16))
    basis = basis.transpose(0, 2, 1).reshape(orders_dev // 2, 2 * kmax, radii)
    rows = kmax // img_size
    pairs = orders_dev // 2
    last = (5 * img_size // 8 + 1) % img_size
    img_order = list(range(img_size))
    img_order[0], img_order[last] = last, 0
    sent = pl.pallas_call(
        functools.partial(covariances, first_of, (last, img_size)),
        out_shape=jax.ShapeDtypeStruct((kmax, pairs, 2 * kmax), BF16),
        in_specs=[vmem, vmem],
        out_specs=vmem,
        scratch_shapes=[
            pltpu.VMEM((lows * lanes, radii), F32),
            pltpu.VMEM((kmax * pairs, 2 * kmax), F32),
        ],
        compiler_params=pltpu.CompilerParams(vmem_limit_bytes=16 * 2**20),
        name="covariances",
    )(parts, basis)
    sent = sent.reshape(img_size, rows * pairs, 2 * kmax)
    got = lax.all_to_all(sent, "img", 0, 0, tiled=True, axis_index_groups=[img_order])
    gram = jnp.sum(got.astype(F32), axis=0)
    return gram.reshape(rows, orders_dev * kmax) * (1.0 / (images_dev * img_size))


def solution(mesh):
    placed = (P("img", "bas", None), P("img"), P(), P("bas", None, None), P("bas"))

    def step(polar_images, ctf_groups, ctf_table, radial_basis, order_counts):
        table = jnp.asarray(angular_table(radial_basis.shape[0], polar_images.shape[2]))
        return jax.shard_map(
            local, mesh=mesh, in_specs=(P(),) + placed, out_specs=P("img", "bas"), check_vma=False
        )(table, polar_images, ctf_groups, ctf_table, radial_basis, order_counts)

    return step
```

time: 803 us -> 51.8 us (0.06)
  the two profiles are of different devices: /device:TPU:128 before, /device:TPU:6 now
where the time goes in v2:
time: 51.8 us; the launch traced here: 50.8 us
  starting transfers between devices  17.6 us (34%)
  blocking collectives  15.6 us (30%)
  waiting for transfers between devices  12.6 us (24%)
  Pallas kernels  3.84 us (7%)
  other arithmetic  0.79 us (2%)
    all_to_all x1, starting transfers between devices, local(): lax.all_to_all(parts, 'bas', 0, 0, tiled=True, axis_index_groups=[bas_ord...  17.6 us
    all_to_all x1, blocking collectives, local(): lax.all_to_all(sent, 'img', 0, 0, tiled=True, axis_index_groups=[img_order])  15.6 us
    all_to_all x1, waiting for transfers between devices, local(): lax.all_to_all(parts, 'bas', 0, 0, tiled=True, axis_index_groups=[bas_ord...  12.6 us
    pallas_call x1, Pallas kernels, local(): pl.pallas_call(functools.partial(transform, first_of), out_shape=jax.Shap...  2.55 us
    pallas_call x1, Pallas kernels, local(): pl.pallas_call(functools.partial(covariances, first_of, (last, img_size))...  1.3 us
  transfers between devices with their start and end apart: 1, of which 1 were waited for; matrix products, arithmetic and copies ran while one was open for 1% of the time, Pallas kernels for 0%

profile of v2, /device:TPU:6, one launch (start us, length us, event | category | flops | bytes accessed | tf_op | source)
XLA Modules:
  0.0 50.8 jit_solution(11286562508216660039)
XLA Ops:
  0.0 0.0 copy-start.1
  0.0 2.5 %transform.1 = bf16[8,128,128]{2,1,0:T(8,128)(2,1)} custom-call(s32[32]{0:T(128)} %groups_in.1, f32[64,64]{1,0:T(8,128)} %ctf_in.1, bf16[256,512]{1,0:T(8,128)(2,1)} %bitcast.6, bf16[2,64,8,256]{3,2,1,0:T(8,128)(2,1)} %constant.8.clone.table_in), custom_call_target="tpu_custom_call" | custom-call | tf_op jit(solution)/shard_map/transform/pallas_call | solution.py:131
  2.6 0.0 copy-start
  2.6 17.6 %all-to-all-start = ((bf16[8,128,128]{2,1,0:T(8,128)(2,1)}), bf16[8,128,128]{2,1,0:T(8,128)(2,1)S(1)}, u32[]{:S(2)}, u32[]{:S(2)}) async-start(bf16[8,128,128]{2,1,0:T(8,128)(2,1)} %transform.1), calls=%async_computation | async-start | bytes 524288 | tf_op jit(solution)/shard_map/all_to_all | solution.py:150
  20.2 0.0 copy-done.1
  20.2 0.1 iota_compare_fusion
  20.3 0.0 copy-done
  20.3 0.3 copy.7
  20.6 12.6 %all-to-all-done.parts_ref = bf16[8,128,128]{2,1,0:T(8,128)(2,1)S(1)} async-done(((bf16[8,128,128]{2,1,0:T(8,128)(2,1)}), bf16[8,128,128]{2,1,0:T(8,128)(2,1)S(1)}, u32[]{:S(2)}, u32[]{:S(2)}) %all-to-all-start) | async-done | bytes 262176 | tf_op jit(solution)/shard_map/all_to_all | solution.py:150
  33.2 1.3 %covariances.1 = bf16[64,16,128]{2,1,0:T(8,128)(2,1)S(1)} custom-call(bf16[8,128,128]{2,1,0:T(8,128)(2,1)S(1)} %all-to-all-done.parts_ref, bf16[16,128,64]{2,1,0:T(8,128)(2,1)S(1)} %bitcast.5), custom_call_target="tpu_custom_call" | custom-call | tf_op jit(solution)/shard_map/covariances/pallas_call | solution.py:159
  34.5 15.6 %all_to_all.10 = bf16[64,16,128]{2,1,0:T(8,128)(2,1)S(1)} all-to-all(bf16[64,16,128]{2,1,0:T(8,128)(2,1)S(1)} %covariances.1), channel_id=1, replica_groups={{328,8,16,24,32,40,48,56,64,72,80,88,96,104,112,120,128,136,144,152,160..., dimensions={0} | all-to-all | bytes 524288 | tf_op jit(solution)/shard_map/all_to_all | solution.py:172
  50.1 0.1 convert_reduce_fusion
  50.2 0.6 %broadcast_multiply_fusion = f32[16,128]{1,0:T(8,128)} fusion(f32[16,128]{1,0:T(8,128)S(1)} %convert_reduce_fusion), kind=kLoop, calls=%fused_computation.3 | loop fusion | flops 2048 | bytes 16384 | tf_op jit(solution)/shard_map/mul | solution.py:174
  (1 shorter events, 0.0 us)
Async XLA Ops:
  0.0 20.2 %copy-start.1 = (s32[32]{0:T(128)S(1)}, s32[32]{0:T(128)}, u32[]{:S(2)}) copy-start(s32[32]{0:T(128)} %param.10) | copy-start | bytes 388
  2.6 17.7 %copy-start = (bf16[32,64,64]{2,1,0:T(8,128)(2,1)S(1)}, bf16[32,64,64]{2,1,0:T(8,128)(2,1)}, u32[]{:S(2)}) copy-start(bf16[32,64,64]{2,1,0:T(8,128)(2,1)} %param.9) | copy-start | bytes 786436
  2.6 30.6 %all-to-all-start = ((bf16[8,128,128]{2,1,0:T(8,128)(2,1)}), bf16[8,128,128]{2,1,0:T(8,128)(2,1)S(1)}, u32[]{:S(2)}, u32[]{:S(2)}) async-start(bf16[8,128,128]{2,1,0:T(8,128)(2,1)} %transform.1), calls=%async_computation | async-start | bytes 524288 | tf_op jit(solution)/shard_map/all_to_all | solution.py:150

commit v3 on v2

--- a/solution.py
+++ b/solution.py
@@ -23,12 +23,13 @@
     return table.astype(ml_dtypes.bfloat16)
 
 
-def transform(first_of, groups_in, ctf_in, images_in, table_in, parts_out, *scratch):
+def transform(place_of, groups_in, ctf_in, images_in, table_in, parts_out, *scratch):
     groups, ctf, images, table, weighted, parts, sem_in, sem_out = scratch
     size, rows, lanes = parts.shape
     classes, radii = ctf.shape
-    radii_dev = radii // size
-    width = lanes // 2
+    radii_dev = weighted.shape[0] // groups.shape[0]
+    highs = weighted.shape[0] // rows
+    width = lanes // highs
     halves = table.shape[0]
     copies = [
         pltpu.make_async_copy(source, target, sem_in.at[n])
@@ -58,49 +59,65 @@
     for n, scale in enumerate(scales):
         block = slice(n * 16, (n + 1) * 16)
         weighted[block, :] = (images[block, :].astype(F32) * scale).astype(BF16)
-    low = lax.broadcasted_iota(jnp.int32, (rows, lanes), 1) < width
-    sends = []
+    group = lax.broadcasted_iota(jnp.int32, (rows, lanes), 1) // width
     for half in range(halves):
         copies[3 + half].wait()
+    for half in range(halves):
         columns = table[half].reshape(weighted.shape[1], -1)
         spectra = jnp.dot(weighted[...], columns, preferred_element_type=F32)
-        for pair in range(columns.shape[1] // lanes):
-            block = spectra[:, pair * lanes : (pair + 1) * lanes]
-            one, two = block[:rows], block[rows:]
-            turned_one, turned_two = pltpu.roll(one, width, 1), pltpu.roll(two, width, 1)
-            for n, value in enumerate((jnp.where(low, one, turned_two), jnp.where(low, turned_one, two))):
-                order = half * (size // halves) + 2 * pair + n
-                place = (order - first_of) % size
+        tiles = columns.shape[1] // lanes
+        for tile in range(tiles):
+            part = spectra[:, tile * lanes : (tile + 1) * lanes]
+            blocks = [part[n * rows : (n + 1) * rows] for n in range(highs)]
+            shift = highs // 2
+            while shift:
+                keep = (group & shift) == 0
+                for n in range(highs):
+                    if not n & shift:
+                        one, two = blocks[n], blocks[n + shift]
+                        turned_one = pltpu.roll(one, lanes - shift * width, 1)
+                        turned_two = pltpu.roll(two, shift * width, 1)
+                        blocks[n] = jnp.where(keep, one, turned_two)
+                        blocks[n + shift] = jnp.where(keep, turned_one, two)
+                shift //= 2
+            for n, value in enumerate(blocks):
+                place = place_of[(half * tiles + tile) * highs + n]
                 parts[place] = value.astype(BF16)
-                send = pltpu.make_async_copy(parts.at[place], parts_out.at[place], sem_out.at[place])
-                send.start()
-                sends.append(send)
-    for send in sends:
-        send.wait()
-
-
-def covariances(first_of, last_of, parts_ref, basis, out, by_order, staged):
-    sources, rows, lanes = parts_ref.shape
+    send = pltpu.make_async_copy(parts, parts_out, sem_out.at[0])
+    send.start()
+    send.wait()
+
+
+def covariances(place_of, last_of, parts_ref, basis, out, by_order, staged):
+    places, rows, lanes = parts_ref.shape
     pairs, wide, radii = basis.shape
+    pool = len(place_of[0])
+    sources = places // pool
     radii_dev = radii // sources
     lows = rows // radii_dev
-    width = lanes // 2
+    width = 4 * pairs
+    highs = lanes // width
     half = wide // 2
     step = 16 // radii_dev
+    blocks = pool * lows
     for i in range(0, lows, step):
         block = parts_ref[:, i * radii_dev : (i + step) * radii_dev, :].astype(F32)
         for j in range(step):
-            one = block[:, j * radii_dev : (j + 1) * radii_dev, :]
-            one = jnp.concatenate([one[(n - first_of) % sources] for n in range(sources)], axis=0)
-            by_order[(i + j) * lanes : (i + j + 1) * lanes, :] = one.T
-    same = (lax.broadcasted_iota(jnp.int32, (wide, wide), 0) < half) == (
-        lax.broadcasted_iota(jnp.int32, (wide, wide), 1) < half
+            for sub in range(pool):
+                at = slice(j * radii_dev, (j + 1) * radii_dev)
+                one = jnp.concatenate([block[place_of[n][sub]][at] for n in range(sources)], axis=0)
+                n = (sub * lows + i + j) * lanes
+                by_order[n : n + lanes, :] = one.T
+    samples = 2 * highs * blocks
+    shape = (wide, 2 * samples)
+    same = (lax.broadcasted_iota(jnp.int32, shape, 0) < half) == (
+        lax.broadcasted_iota(jnp.int32, shape, 1) < samples
     )
     for pair in range(pairs):
         rows_of = [
-            by_order[pl.ds(high * width + 4 * pair + 2 * order + c, lows, stride=lanes), :]
+            by_order[pl.ds(high * width + 4 * pair + 2 * order + c, blocks, stride=lanes), :]
             for order in range(2)
-            for high in range(2)
+            for high in range(highs)
             for c in range(2)
         ]
         spectra = jnp.concatenate(rows_of, axis=0).astype(BF16)
@@ -122,14 +139,22 @@
     img_size, bas_size = lax.axis_size("img"), lax.axis_size("bas")
     hbm = pl.BlockSpec(memory_space=pltpu.HBM)
     vmem = pl.BlockSpec(memory_space=pltpu.VMEM)
-    lows = images_dev // 2
-    lanes = 4 * orders_dev
-    shape = (bas_size, lows * radii_dev, lanes)
-    first_of = bas_size // 2
-    bas_order = [(n + first_of) % bas_size for n in range(bas_size)]
+    pool = 2
+    lanes = 128
+    lows = images_dev * orders_dev * 2 // pool // lanes
+    places = bas_size * pool
+    shape = (places, lows * radii_dev, lanes)
+    ring = [(high, sub, core) for high in range(bas_size // 2) for sub in range(pool) for core in range(2)]
+    start = places // 2
+    ring = ring[start:] + ring[:start]
+    members = [(sub, 2 * high + core) for high, sub, core in ring]
+    place_of = [[members.index((sub, bas)) for sub in range(pool)] for bas in range(bas_size)]
+    teams = [
+        [(team * pool + sub) * bas_size + bas for sub, bas in members] for team in range(img_size // pool)
+    ]
     images = polar_images.reshape(-1, angles)
     parts = pl.pallas_call(
-        functools.partial(transform, first_of),
+        functools.partial(transform, sum(place_of, [])),
         out_shape=jax.ShapeDtypeStruct(shape, BF16),
         in_specs=[hbm] * 4,
         out_specs=hbm,
@@ -141,28 +166,32 @@
             pltpu.VMEM(images.shape, BF16),
             pltpu.VMEM(shape, BF16),
             pltpu.SemaphoreType.DMA((3 + table.shape[0],)),
-            pltpu.SemaphoreType.DMA((bas_size,)),
+            pltpu.SemaphoreType.DMA((1,)),
         ],
         compiler_params=pltpu.CompilerParams(vmem_limit_bytes=60 * 2**20),
         name="transform",
     )(ctf_groups, ctf_table, images, table)
     parts, radial_basis, order_counts = lax.optimization_barrier((parts, radial_basis, order_counts))
-    parts = lax.all_to_all(parts, "bas", 0, 0, tiled=True, axis_index_groups=[bas_order])
-    kept = jnp.arange(kmax, dtype=jnp.int32)[None, :] < order_counts[:, None]
-    basis = jnp.where(kept[:, None, :], radial_basis, jnp.zeros((), BF16))
-    basis = basis.transpose(0, 2, 1).reshape(orders_dev // 2, 2 * kmax, radii)
+    parts = lax.all_to_all(parts, ("img", "bas"), 0, 0, tiled=True, axis_index_groups=teams)
+    orders = orders_dev // pool
+    mine = lax.axis_index("img") % pool * orders
+    counts = lax.dynamic_slice_in_dim(order_counts, mine, orders)
+    basis = lax.dynamic_slice_in_dim(radial_basis, mine, orders)
+    kept = jnp.arange(kmax, dtype=jnp.int32)[None, :] < counts[:, None]
+    basis = jnp.where(kept[:, None, :], basis, jnp.zeros((), BF16))
+    basis = basis.transpose(0, 2, 1).reshape(orders // 2, 2 * kmax, radii)
     rows = kmax // img_size
-    pairs = orders_dev // 2
-    last = (5 * img_size // 8 + 1) % img_size
+    pairs = orders // 2
+    last = img_size // 64 * 42
     img_order = list(range(img_size))
     img_order[0], img_order[last] = last, 0
     sent = pl.pallas_call(
-        functools.partial(covariances, first_of, (last, img_size)),
+        functools.partial(covariances, place_of, (last, img_size)),
         out_shape=jax.ShapeDtypeStruct((kmax, pairs, 2 * kmax), BF16),
         in_specs=[vmem, vmem],
         out_specs=vmem,
         scratch_shapes=[
-            pltpu.VMEM((lows * lanes, radii), F32),
+            pltpu.VMEM((pool * lows * lanes, radii), F32),
             pltpu.VMEM((kmax * pairs, 2 * kmax), F32),
         ],
         compiler_params=pltpu.CompilerParams(vmem_limit_bytes=16 * 2**20),
@@ -170,7 +199,8 @@
     )(parts, basis)
     sent = sent.reshape(img_size, rows * pairs, 2 * kmax)
     got = lax.all_to_all(sent, "img", 0, 0, tiled=True, axis_index_groups=[img_order])
-    gram = jnp.sum(got.astype(F32), axis=0)
+    got = got.astype(F32).reshape(img_size // pool, pool, rows, pairs, 2 * kmax)
+    gram = jnp.sum(got, axis=0).swapaxes(0, 1)
     return gram.reshape(rows, orders_dev * kmax) * (1.0 / (images_dev * img_size))
 
 

time: 51.8 us -> 50.3 us (0.971)
  blocking collectives: 15.6 us -> 14.4 us
  waiting for transfers between devices: 12.6 us -> 11.8 us
  local copies, waits for them, and re-layouts: 0.28 us -> 0.9 us
    all_to_all x1, blocking collectives: 15.6 us -> 14.4 us  [local(): lax.all_to_all(sent, 'img', 0, 0, tiled=True, axis_index_groups=[img_order])]
    all_to_all x1, waiting for transfers between devices: 12.6 us -> 11.8 us  [local(): lax.all_to_all(parts, ('img', 'bas'), 0, 0, tiled=True, axis_index_groups...]
    unnamed x4, local copies, waits for them, and re-layouts: 0.01 us -> 0.65 us
where the time goes in v3:
time: 50.3 us; the launch traced here: 49.4 us
  starting transfers between devices  18.1 us (36%)
  blocking collectives  14.4 us (29%)
  waiting for transfers between devices  11.8 us (23%)
  Pallas kernels  3.45 us (7%)
  local copies, waits for them, and re-layouts  0.9 us (2%)
  other arithmetic  0.74 us (1%)
    all_to_all x1, starting transfers between devices, local(): lax.all_to_all(parts, ('img', 'bas'), 0, 0, tiled=True, axis_index_groups...  18.1 us
    all_to_all x1, blocking collectives, local(): lax.all_to_all(sent, 'img', 0, 0, tiled=True, axis_index_groups=[img_order])  14.4 us
    all_to_all x1, waiting for transfers between devices, local(): lax.all_to_all(parts, ('img', 'bas'), 0, 0, tiled=True, axis_index_groups...  11.8 us
    pallas_call x1, Pallas kernels, local(): pl.pallas_call(functools.partial(transform, sum(place_of, [])), out_shape...  2.32 us
    pallas_call x1, Pallas kernels, local(): pl.pallas_call(functools.partial(covariances, place_of, (last, img_size))...  1.13 us
  transfers between devices with their start and end apart: 1, of which 1 were waited for; matrix products, arithmetic and copies ran while one was open for 1% of the time, Pallas kernels for 0%

profile of v3, /device:TPU:6, one launch (start us, length us, event | category | flops | bytes accessed | tf_op | source)
XLA Modules:
  0.0 49.4 jit_solution(16078794034590364450)
XLA Ops:
  0.0 2.3 %transform.1 = bf16[16,64,128]{2,1,0:T(8,128)(2,1)} custom-call(s32[32]{0:T(128)} %groups_in.1, f32[64,64]{1,0:T(8,128)} %ctf_in.1, bf16[256,512]{1,0:T(8,128)(2,1)} %bitcast.9, bf16[2,64,8,256]{3,2,1,0:T(8,128)(2,1)} %constant.32.clone.table_in), custom_call_target="tpu_custom_call" | custom-call | tf_op jit(solution)/shard_map/transform/pallas_call | solution.py:156
  2.3 0.0 copy-start
  2.3 18.1 %all-to-all-start = ((bf16[16,64,128]{2,1,0:T(8,128)(2,1)}), bf16[16,64,128]{2,1,0:T(8,128)(2,1)S(1)}, u32[]{:S(2)}, u32[]{:S(2)}) async-start(bf16[16,64,128]{2,1,0:T(8,128)(2,1)} %transform.1), calls=%async_computation | async-start | bytes 524288 | tf_op jit(solution)/shard_map/all_to_all | solution.py:175
  20.4 0.0 copy-start.1
  20.4 0.6 %copy-done.1 = s32[32]{0:T(128)S(1)} copy-done((s32[32]{0:T(128)S(1)}, s32[32]{0:T(128)}, u32[]{:S(2)}) %copy-start.1) | copy-done | bytes 152
  21.1 0.1 dynamic_slice.6
  21.2 0.1 iota_compare_fusion
  21.2 0.0 copy-done
  21.3 0.2 copy.7
  21.4 11.8 %all-to-all-done.parts_ref = bf16[16,64,128]{2,1,0:T(8,128)(2,1)S(1)} async-done(((bf16[16,64,128]{2,1,0:T(8,128)(2,1)}), bf16[16,64,128]{2,1,0:T(8,128)(2,1)S(1)}, u32[]{:S(2)}, u32[]{:S(2)}) %all-to-all-start) | async-done | bytes 262176 | tf_op jit(solution)/shard_map/all_to_all | solution.py:175
  33.2 1.1 %covariances.1 = bf16[64,8,128]{2,1,0:T(8,128)(2,1)S(1)} custom-call(bf16[16,64,128]{2,1,0:T(8,128)(2,1)S(1)} %all-to-all-done.parts_ref, bf16[8,128,64]{2,1,0:T(8,128)(2,1)S(1)} %bitcast.7), custom_call_target="tpu_custom_call" | custom-call | tf_op jit(solution)/shard_map/covariances/pallas_call | solution.py:188
  34.3 14.4 %all_to_all.10 = bf16[64,8,128]{2,1,0:T(8,128)(2,1)S(1)} all-to-all(bf16[64,8,128]{2,1,0:T(8,128)(2,1)S(1)} %covariances.1), channel_id=1, replica_groups={{336,8,16,24,32,40,48,56,64,72,80,88,96,104,112,120,128,136,144,152,160..., dimensions={0} | all-to-all | bytes 262144 | tf_op jit(solution)/shard_map/all_to_all | solution.py:201
  48.8 0.6 %broadcast_multiply_fusion = f32[2,8,128]{2,1,0:T(8,128)} fusion(f32[2,8,128]{2,1,0:T(8,128)S(1)} %convert_reduce_fusion), kind=kLoop, calls=%fused_computation.3 | loop fusion | flops 2048 | bytes 16384 | tf_op jit(solution)/shard_map/mul | solution.py:204
  (2 shorter events, 0.1 us)
Async XLA Ops:
  2.3 18.9 %copy-start = (bf16[32,64,64]{2,1,0:T(8,128)(2,1)S(1)}, bf16[32,64,64]{2,1,0:T(8,128)(2,1)}, u32[]{:S(2)}) copy-start(bf16[32,64,64]{2,1,0:T(8,128)(2,1)} %param.9) | copy-start | bytes 786436
  2.3 30.9 %all-to-all-start = ((bf16[16,64,128]{2,1,0:T(8,128)(2,1)}), bf16[16,64,128]{2,1,0:T(8,128)(2,1)S(1)}, u32[]{:S(2)}, u32[]{:S(2)}) async-start(bf16[16,64,128]{2,1,0:T(8,128)(2,1)} %transform.1), calls=%async_computation | async-start | bytes 524288 | tf_op jit(solution)/shard_map/all_to_all | solution.py:175
  20.4 0.7 %copy-start.1 = (s32[32]{0:T(128)S(1)}, s32[32]{0:T(128)}, u32[]{:S(2)}) copy-start(s32[32]{0:T(128)} %param.10) | copy-start | bytes 388

commit v4 on v3

--- a/solution.py
+++ b/solution.py
@@ -88,7 +88,7 @@
     send.wait()
 
 
-def covariances(place_of, last_of, parts_ref, basis, out, by_order, staged):
+def covariances(place_of, chunk_of, parts_ref, basis, out, by_order, staged):
     places, rows, lanes = parts_ref.shape
     pairs, wide, radii = basis.shape
     pool = len(place_of[0])
@@ -125,12 +125,10 @@
         coeffs = jnp.where(same, coeffs, 0.0).astype(BF16)
         gram = lax.dot_general(coeffs, coeffs, NT, preferred_element_type=F32)
         staged[pl.ds(pair, half, stride=pairs), :] = gram[:half] + gram[half:]
-    grams = staged[...].astype(BF16).reshape(out.shape)
-    out[...] = grams
-    if last_of:
-        chunk = out.shape[0] // last_of[1]
-        for here, there in ((0, last_of[0]), (last_of[0], 0)):
-            out[here * chunk : (here + 1) * chunk] = grams[there * chunk : (there + 1) * chunk]
+    count = len(chunk_of)
+    chunk = out.shape[0] // count
+    for here in range(count):
+        out[here * chunk : (here + 1) * chunk, :] = staged[chunk_of[here] * chunk : (chunk_of[here] + 1) * chunk, :]
 
 
 def local(table, polar_images, ctf_groups, ctf_table, radial_basis, order_counts):
@@ -139,13 +137,13 @@
     img_size, bas_size = lax.axis_size("img"), lax.axis_size("bas")
     hbm = pl.BlockSpec(memory_space=pltpu.HBM)
     vmem = pl.BlockSpec(memory_space=pltpu.VMEM)
-    pool = 2
+    pool = 4
     lanes = 128
     lows = images_dev * orders_dev * 2 // pool // lanes
     places = bas_size * pool
     shape = (places, lows * radii_dev, lanes)
     ring = [(high, sub, core) for high in range(bas_size // 2) for sub in range(pool) for core in range(2)]
-    start = places // 2
+    start = 5 * places // 8
     ring = ring[start:] + ring[:start]
     members = [(sub, 2 * high + core) for high, sub, core in ring]
     place_of = [[members.index((sub, bas)) for sub in range(pool)] for bas in range(bas_size)]
@@ -182,12 +180,10 @@
     basis = basis.transpose(0, 2, 1).reshape(orders // 2, 2 * kmax, radii)
     rows = kmax // img_size
     pairs = orders // 2
-    last = img_size // 64 * 42
-    img_order = list(range(img_size))
-    img_order[0], img_order[last] = last, 0
+    img_order = [n ^ (img_size // 64 * 42) for n in range(img_size)]
     sent = pl.pallas_call(
-        functools.partial(covariances, place_of, (last, img_size)),
-        out_shape=jax.ShapeDtypeStruct((kmax, pairs, 2 * kmax), BF16),
+        functools.partial(covariances, place_of, img_order),
+        out_shape=jax.ShapeDtypeStruct((kmax * pairs, 2 * kmax), F32),
         in_specs=[vmem, vmem],
         out_specs=vmem,
         scratch_shapes=[
@@ -199,8 +195,8 @@
     )(parts, basis)
     sent = sent.reshape(img_size, rows * pairs, 2 * kmax)
     got = lax.all_to_all(sent, "img", 0, 0, tiled=True, axis_index_groups=[img_order])
-    got = got.astype(F32).reshape(img_size // pool, pool, rows, pairs, 2 * kmax)
-    gram = jnp.sum(got, axis=0).swapaxes(0, 1)
+    gram = jnp.sum(got.reshape(img_size // pool, pool, rows, pairs, 2 * kmax), axis=0)
+    gram = jnp.stack([gram[img_order[n] % pool] for n in range(pool)], axis=1)
     return gram.reshape(rows, orders_dev * kmax) * (1.0 / (images_dev * img_size))
 
 

time: 50.3 us -> 51.2 us (1.018)
  blocking collectives: 14.4 us -> 15.4 us
  starting transfers between devices: 18.1 us -> 17.2 us
  other arithmetic: 0.74 us -> 1.64 us
    all_to_all x1, blocking collectives: 14.4 us -> 15.4 us  [local(): lax.all_to_all(sent, 'img', 0, 0, tiled=True, axis_index_groups=[img_order])]
    transpose x1, other arithmetic: 0.03 us -> 0.92 us  [local(): basis = basis.transpose(0, 2, 1).reshape(orders // 2, 2 * kmax, radii)]
    all_to_all x1, starting transfers between devices: 18.1 us -> 17.2 us  [local(): lax.all_to_all(parts, ('img', 'bas'), 0, 0, tiled=True, axis_index_groups...]
  transfers between devices with their start and end apart: 1 -> 1, of which waited for: 1 -> 1; matrix products, arithmetic and copies ran while one was open for 1% -> 2% of each run, Pallas kernels for 0% -> 0%
where the time goes in v4:
time: 51.2 us; the launch traced here: 50.4 us
  starting transfers between devices  17.2 us (34%)
  blocking collectives  15.4 us (30%)
  waiting for transfers between devices  11.7 us (23%)
  Pallas kernels  3.51 us (7%)
  other arithmetic  1.64 us (3%)
  local copies, waits for them, and re-layouts  0.85 us (2%)
    all_to_all x1, starting transfers between devices, local(): lax.all_to_all(parts, ('img', 'bas'), 0, 0, tiled=True, axis_index_groups...  17.2 us
    all_to_all x1, blocking collectives, local(): lax.all_to_all(sent, 'img', 0, 0, tiled=True, axis_index_groups=[img_order])  15.4 us
    all_to_all x1, waiting for transfers between devices, local(): lax.all_to_all(parts, ('img', 'bas'), 0, 0, tiled=True, axis_index_groups...  11.7 us
    pallas_call x1, Pallas kernels, local(): pl.pallas_call(functools.partial(transform, sum(place_of, [])), out_shape...  2.39 us
    pallas_call x1, Pallas kernels, local(): pl.pallas_call(functools.partial(covariances, place_of, img_order), out_s...  1.12 us
  transfers between devices with their start and end apart: 1, of which 1 were waited for; matrix products, arithmetic and copies ran while one was open for 2% of the time, Pallas kernels for 0%

profile of v4, /device:TPU:6, one launch (start us, length us, event | category | flops | bytes accessed | tf_op | source)
XLA Modules:
  0.0 50.4 jit_solution(1811647865289049632)
XLA Ops:
  0.0 2.4 %transform.1 = bf16[32,32,128]{2,1,0:T(8,128)(2,1)} custom-call(s32[32]{0:T(128)} %groups_in.1, f32[64,64]{1,0:T(8,128)} %ctf_in.1, bf16[256,512]{1,0:T(8,128)(2,1)} %bitcast.18, bf16[2,64,8,256]{3,2,1,0:T(8,128)(2,1)} %constant.32.clone.table_in), custom_call_target="tpu_custom_call" | custom-call | tf_op jit(solution)/shard_map/transform/pallas_call | solution.py:154
  2.4 17.2 %all-to-all-start = ((bf16[32,32,128]{2,1,0:T(8,128)(2,1)}), bf16[32,32,128]{2,1,0:T(8,128)(2,1)S(1)}, u32[]{:S(2)}, u32[]{:S(2)}) async-start(bf16[32,32,128]{2,1,0:T(8,128)(2,1)} %transform.1), calls=%async_computation | async-start | bytes 524288 | tf_op jit(solution)/shard_map/all_to_all | solution.py:173
  19.6 0.0 copy-start
  19.6 0.6 %copy-done = s32[32]{0:T(128)S(1)} copy-done((s32[32]{0:T(128)S(1)}, s32[32]{0:T(128)}, u32[]{:S(2)}) %copy-start) | copy-done | bytes 152
  20.3 0.1 dynamic_slice.6
  20.4 0.1 iota_compare_fusion
  20.4 0.9 %select_bitcast_fusion = bf16[8,64,64]{1,2,0:T(8,128)(2,1)S(1)} fusion(bf16[32,64,64]{2,1,0:T(8,128)(2,1)} %param.9, s32[]{:T(128)S(6)} %select_n.16, pred[8,64]{1,0:T(8,128)(4,1)S(1)} %iota_compare_fusion), kind=kLoop, calls=%fused_computation | loop fusion | flops 32768 | bytes 131588 | tf_op jit(solution)/shard_map/transpose | solution.py:180
  21.4 0.1 copy.7
  21.5 11.7 %all-to-all-done.parts_ref = bf16[32,32,128]{2,1,0:T(8,128)(2,1)S(1)} async-done(((bf16[32,32,128]{2,1,0:T(8,128)(2,1)}), bf16[32,32,128]{2,1,0:T(8,128)(2,1)S(1)}, u32[]{:S(2)}, u32[]{:S(2)}) %all-to-all-start) | async-done | bytes 262176 | tf_op jit(solution)/shard_map/all_to_all | solution.py:173
  33.2 1.1 %covariances.1 = f32[256,128]{1,0:T(8,128)S(1)} custom-call(bf16[32,32,128]{2,1,0:T(8,128)(2,1)S(1)} %all-to-all-done.parts_ref, bf16[4,128,64]{2,1,0:T(8,128)(2,1)S(1)} %bitcast.15), custom_call_target="tpu_custom_call" | custom-call | tf_op jit(solution)/shard_map/covariances/pallas_call | solution.py:184
  34.4 15.4 %all_to_all.10 = f32[64,4,128]{2,1,0:T(4,128)S(1)} all-to-all(f32[64,4,128]{2,1,0:T(4,128)S(1)} %bitcast.16), channel_id=1, replica_groups={{336,344,320,328,368,376,352,360,272,280,256,264,304,312,288,296,464,47..., dimensions={0} | all-to-all | bytes 262144 | tf_op jit(solution)/shard_map/all_to_all | solution.py:197
  49.8 0.6 %maximum_multiply_fusion = f32[1,4,4,128]{3,2,1,0:T(4,128)} fusion(f32[1,1,4,128]{3,2,1,0:T(4,128)S(1)} %get-tuple-element.12, f32[1,1,4,128]{3,2,1,0:T(4,128)S(1)} %get-tuple-element.13, f32[1,1,4,128]{3,2,1,0:T(4,128)S(1)} %get-tuple-element.14, f32[1,1,4,128]{3,2,1,0:T(4,128)S(1)} %get-tuple-element.11), kind=kLoop, calls=%fused_computation.1 | loop fusion | flops 8192 | bytes 16384 | tf_op jit(solution)/shard_map/mul | solution.py:200
  (2 shorter events, 0.0 us)
Async XLA Ops:
  2.4 30.8 %all-to-all-start = ((bf16[32,32,128]{2,1,0:T(8,128)(2,1)}), bf16[32,32,128]{2,1,0:T(8,128)(2,1)S(1)}, u32[]{:S(2)}, u32[]{:S(2)}) async-start(bf16[32,32,128]{2,1,0:T(8,128)(2,1)} %transform.1), calls=%async_computation | async-start | bytes 524288 | tf_op jit(solution)/shard_map/all_to_all | solution.py:173
  19.6 0.7 %copy-start = (s32[32]{0:T(128)S(1)}, s32[32]{0:T(128)}, u32[]{:S(2)}) copy-start(s32[32]{0:T(128)} %param.10) | copy-start | bytes 388

commit v5 on v4

--- a/solution.py
+++ b/solution.py
@@ -125,10 +125,11 @@
         coeffs = jnp.where(same, coeffs, 0.0).astype(BF16)
         gram = lax.dot_general(coeffs, coeffs, NT, preferred_element_type=F32)
         staged[pl.ds(pair, half, stride=pairs), :] = gram[:half] + gram[half:]
-    count = len(chunk_of)
-    chunk = out.shape[0] // count
+    count = len(chunk_of) // 2
+    step = out.shape[0] // count
     for here in range(count):
-        out[here * chunk : (here + 1) * chunk, :] = staged[chunk_of[here] * chunk : (chunk_of[here] + 1) * chunk, :]
+        there = chunk_of[2 * here] // 2
+        out[here * step : (here + 1) * step, :] = staged[there * step : (there + 1) * step, :]
 
 
 def local(table, polar_images, ctf_groups, ctf_table, radial_basis, order_counts):
@@ -187,8 +188,8 @@
         in_specs=[vmem, vmem],
         out_specs=vmem,
         scratch_shapes=[
-            pltpu.VMEM((pool * lows * lanes, radii), F32),
-            pltpu.VMEM((kmax * pairs, 2 * kmax), F32),
+            pltpu.VMEM(((pool * lows + 1) * lanes, radii), F32),
+            pltpu.VMEM((kmax * pairs + 8, 2 * kmax), F32),
         ],
         compiler_params=pltpu.CompilerParams(vmem_limit_bytes=16 * 2**20),
         name="covariances",

time: 51.2 us -> 51.2 us (level)
  no operation moved by 1% of the time
where the time goes in v5:
time: 51.2 us; the launch traced here: 50.4 us
  starting transfers between devices  17.2 us (34%)
  blocking collectives  15.4 us (30%)
  waiting for transfers between devices  11.7 us (23%)
  Pallas kernels  3.51 us (7%)
  other arithmetic  1.64 us (3%)
  local copies, waits for them, and re-layouts  0.85 us (2%)
    all_to_all x1, starting transfers between devices, local(): lax.all_to_all(parts, ('img', 'bas'), 0, 0, tiled=True, axis_index_groups...  17.2 us
    all_to_all x1, blocking collectives, local(): lax.all_to_all(sent, 'img', 0, 0, tiled=True, axis_index_groups=[img_order])  15.4 us
    all_to_all x1, waiting for transfers between devices, local(): lax.all_to_all(parts, ('img', 'bas'), 0, 0, tiled=True, axis_index_groups...  11.7 us
    pallas_call x1, Pallas kernels, local(): pl.pallas_call(functools.partial(transform, sum(place_of, [])), out_shape...  2.39 us
    pallas_call x1, Pallas kernels, local(): pl.pallas_call(functools.partial(covariances, place_of, img_order), out_s...  1.12 us
  transfers between devices with their start and end apart: 1, of which 1 were waited for; matrix products, arithmetic and copies ran while one was open for 2% of the time, Pallas kernels for 0%

profile of v5, /device:TPU:6, one launch (start us, length us, event | category | flops | bytes accessed | tf_op | source)
XLA Modules:
  0.0 50.4 jit_solution(5273417443549539111)
XLA Ops:
  0.0 2.4 %transform.1 = bf16[32,32,128]{2,1,0:T(8,128)(2,1)} custom-call(s32[32]{0:T(128)} %groups_in.1, f32[64,64]{1,0:T(8,128)} %ctf_in.1, bf16[256,512]{1,0:T(8,128)(2,1)} %bitcast.18, bf16[2,64,8,256]{3,2,1,0:T(8,128)(2,1)} %constant.32.clone.table_in), custom_call_target="tpu_custom_call" | custom-call | tf_op jit(solution)/shard_map/transform/pallas_call | solution.py:155
  2.4 17.2 %all-to-all-start = ((bf16[32,32,128]{2,1,0:T(8,128)(2,1)}), bf16[32,32,128]{2,1,0:T(8,128)(2,1)S(1)}, u32[]{:S(2)}, u32[]{:S(2)}) async-start(bf16[32,32,128]{2,1,0:T(8,128)(2,1)} %transform.1), calls=%async_computation | async-start | bytes 524288 | tf_op jit(solution)/shard_map/all_to_all | solution.py:174
  19.6 0.0 copy-start
  19.6 0.6 %copy-done = s32[32]{0:T(128)S(1)} copy-done((s32[32]{0:T(128)S(1)}, s32[32]{0:T(128)}, u32[]{:S(2)}) %copy-start) | copy-done | bytes 152
  20.3 0.1 dynamic_slice.6
  20.4 0.1 iota_compare_fusion
  20.4 0.9 %select_bitcast_fusion = bf16[8,64,64]{1,2,0:T(8,128)(2,1)S(1)} fusion(bf16[32,64,64]{2,1,0:T(8,128)(2,1)} %param.9, s32[]{:T(128)S(6)} %select_n.16, pred[8,64]{1,0:T(8,128)(4,1)S(1)} %iota_compare_fusion), kind=kLoop, calls=%fused_computation | loop fusion | flops 32768 | bytes 131588 | tf_op jit(solution)/shard_map/transpose | solution.py:181
  21.4 0.1 copy.7
  21.5 11.7 %all-to-all-done.parts_ref = bf16[32,32,128]{2,1,0:T(8,128)(2,1)S(1)} async-done(((bf16[32,32,128]{2,1,0:T(8,128)(2,1)}), bf16[32,32,128]{2,1,0:T(8,128)(2,1)S(1)}, u32[]{:S(2)}, u32[]{:S(2)}) %all-to-all-start) | async-done | bytes 262176 | tf_op jit(solution)/shard_map/all_to_all | solution.py:174
  33.2 1.1 %covariances.1 = f32[256,128]{1,0:T(8,128)S(1)} custom-call(bf16[32,32,128]{2,1,0:T(8,128)(2,1)S(1)} %all-to-all-done.parts_ref, bf16[4,128,64]{2,1,0:T(8,128)(2,1)S(1)} %bitcast.15), custom_call_target="tpu_custom_call" | custom-call | tf_op jit(solution)/shard_map/covariances/pallas_call | solution.py:185
  34.4 15.4 %all_to_all.10 = f32[64,4,128]{2,1,0:T(4,128)S(1)} all-to-all(f32[64,4,128]{2,1,0:T(4,128)S(1)} %bitcast.16), channel_id=1, replica_groups={{336,344,320,328,368,376,352,360,272,280,256,264,304,312,288,296,464,47..., dimensions={0} | all-to-all | bytes 262144 | tf_op jit(solution)/shard_map/all_to_all | solution.py:198
  49.8 0.6 %maximum_multiply_fusion = f32[1,4,4,128]{3,2,1,0:T(4,128)} fusion(f32[1,1,4,128]{3,2,1,0:T(4,128)S(1)} %get-tuple-element.12, f32[1,1,4,128]{3,2,1,0:T(4,128)S(1)} %get-tuple-element.13, f32[1,1,4,128]{3,2,1,0:T(4,128)S(1)} %get-tuple-element.14, f32[1,1,4,128]{3,2,1,0:T(4,128)S(1)} %get-tuple-element.11), kind=kLoop, calls=%fused_computation.1 | loop fusion | flops 8192 | bytes 16384 | tf_op jit(solution)/shard_map/mul | solution.py:201
  (2 shorter events, 0.0 us)
Async XLA Ops:
  2.4 30.8 %all-to-all-start = ((bf16[32,32,128]{2,1,0:T(8,128)(2,1)}), bf16[32,32,128]{2,1,0:T(8,128)(2,1)S(1)}, u32[]{:S(2)}, u32[]{:S(2)}) async-start(bf16[32,32,128]{2,1,0:T(8,128)(2,1)} %transform.1), calls=%async_computation | async-start | bytes 524288 | tf_op jit(solution)/shard_map/all_to_all | solution.py:174
  19.6 0.7 %copy-start = (s32[32]{0:T(128)S(1)}, s32[32]{0:T(128)}, u32[]{:S(2)}) copy-start(s32[32]{0:T(128)} %param.10) | copy-start | bytes 388

commit v6 on v5

--- a/solution.py
+++ b/solution.py
@@ -62,6 +62,7 @@
     group = lax.broadcasted_iota(jnp.int32, (rows, lanes), 1) // width
     for half in range(halves):
         copies[3 + half].wait()
+    sends = []
     for half in range(halves):
         columns = table[half].reshape(weighted.shape[1], -1)
         spectra = jnp.dot(weighted[...], columns, preferred_element_type=F32)
@@ -83,9 +84,15 @@
             for n, value in enumerate(blocks):
                 place = place_of[(half * tiles + tile) * highs + n]
                 parts[place] = value.astype(BF16)
-    send = pltpu.make_async_copy(parts, parts_out, sem_out.at[0])
-    send.start()
-    send.wait()
+        span = size // halves
+        begin = min(place_of[half * span : (half + 1) * span])
+        send = pltpu.make_async_copy(
+            parts.at[pl.ds(begin, span)], parts_out.at[pl.ds(begin, span)], sem_out.at[half]
+        )
+        send.start()
+        sends.append(send)
+    for send in sends:
+        send.wait()
 
 
 def covariances(place_of, chunk_of, parts_ref, basis, out, by_order, staged):
@@ -144,7 +151,7 @@
     places = bas_size * pool
     shape = (places, lows * radii_dev, lanes)
     ring = [(high, sub, core) for high in range(bas_size // 2) for sub in range(pool) for core in range(2)]
-    start = 5 * places // 8
+    start = places // 2
     ring = ring[start:] + ring[:start]
     members = [(sub, 2 * high + core) for high, sub, core in ring]
     place_of = [[members.index((sub, bas)) for sub in range(pool)] for bas in range(bas_size)]
@@ -165,7 +172,7 @@
             pltpu.VMEM(images.shape, BF16),
             pltpu.VMEM(shape, BF16),
             pltpu.SemaphoreType.DMA((3 + table.shape[0],)),
-            pltpu.SemaphoreType.DMA((1,)),
+            pltpu.SemaphoreType.DMA((table.shape[0],)),
         ],
         compiler_params=pltpu.CompilerParams(vmem_limit_bytes=60 * 2**20),
         name="transform",

time: 51.2 us -> 51.7 us (level); the launches traced: 50.4 us -> 51.5 us
  starting transfers between devices: 17.2 us -> 19 us
  waiting for transfers between devices: 11.7 us -> 10.7 us
    all_to_all x1, starting transfers between devices: 17.2 us -> 19 us  [local(): lax.all_to_all(parts, ('img', 'bas'), 0, 0, tiled=True, axis_index_groups...]
    all_to_all x1, waiting for transfers between devices: 11.7 us -> 10.7 us  [local(): lax.all_to_all(parts, ('img', 'bas'), 0, 0, tiled=True, axis_index_groups...]
where the time goes in v6:
time: 51.7 us; the launch traced here: 51.5 us
  starting transfers between devices  19 us (37%)
  blocking collectives  15.7 us (30%)
  waiting for transfers between devices  10.7 us (21%)
  Pallas kernels  3.52 us (7%)
  other arithmetic  1.64 us (3%)
  local copies, waits for them, and re-layouts  0.85 us (2%)
    all_to_all x1, starting transfers between devices, local(): lax.all_to_all(parts, ('img', 'bas'), 0, 0, tiled=True, axis_index_groups...  19 us
    all_to_all x1, blocking collectives, local(): lax.all_to_all(sent, 'img', 0, 0, tiled=True, axis_index_groups=[img_order])  15.7 us
    all_to_all x1, waiting for transfers between devices, local(): lax.all_to_all(parts, ('img', 'bas'), 0, 0, tiled=True, axis_index_groups...  10.7 us
    pallas_call x1, Pallas kernels, local(): pl.pallas_call(functools.partial(transform, sum(place_of, [])), out_shape...  2.41 us
    pallas_call x1, Pallas kernels, local(): pl.pallas_call(functools.partial(covariances, place_of, img_order), out_s...  1.11 us
  transfers between devices with their start and end apart: 1, of which 1 were waited for; matrix products, arithmetic and copies ran while one was open for 2% of the time, Pallas kernels for 0%

profile of v6, /device:TPU:6, one launch (start us, length us, event | category | flops | bytes accessed | tf_op | source)
XLA Modules:
  0.0 51.5 jit_solution(14049335941990880958)
XLA Ops:
  0.0 2.4 %transform.1 = bf16[32,32,128]{2,1,0:T(8,128)(2,1)} custom-call(s32[32]{0:T(128)} %groups_in.1, f32[64,64]{1,0:T(8,128)} %ctf_in.1, bf16[256,512]{1,0:T(8,128)(2,1)} %bitcast.18, bf16[2,64,8,256]{3,2,1,0:T(8,128)(2,1)} %constant.32.clone.table_in), custom_call_target="tpu_custom_call" | custom-call | tf_op jit(solution)/shard_map/transform/pallas_call | solution.py:162
  2.4 19.0 %all-to-all-start = ((bf16[32,32,128]{2,1,0:T(8,128)(2,1)}), bf16[32,32,128]{2,1,0:T(8,128)(2,1)S(1)}, u32[]{:S(2)}, u32[]{:S(2)}) async-start(bf16[32,32,128]{2,1,0:T(8,128)(2,1)} %transform.1), calls=%async_computation | async-start | bytes 524288 | tf_op jit(solution)/shard_map/all_to_all | solution.py:181
  21.4 0.0 copy-start
  21.5 0.6 %copy-done = s32[32]{0:T(128)S(1)} copy-done((s32[32]{0:T(128)S(1)}, s32[32]{0:T(128)}, u32[]{:S(2)}) %copy-start) | copy-done | bytes 152
  22.1 0.1 dynamic_slice.6
  22.2 0.1 iota_compare_fusion
  22.3 0.9 %select_bitcast_fusion = bf16[8,64,64]{1,2,0:T(8,128)(2,1)S(1)} fusion(bf16[32,64,64]{2,1,0:T(8,128)(2,1)} %param.9, s32[]{:T(128)S(6)} %select_n.16, pred[8,64]{1,0:T(8,128)(4,1)S(1)} %iota_compare_fusion), kind=kLoop, calls=%fused_computation | loop fusion | flops 32768 | bytes 131588 | tf_op jit(solution)/shard_map/transpose | solution.py:188
  23.2 0.1 copy.7
  23.3 10.7 %all-to-all-done.parts_ref = bf16[32,32,128]{2,1,0:T(8,128)(2,1)S(1)} async-done(((bf16[32,32,128]{2,1,0:T(8,128)(2,1)}), bf16[32,32,128]{2,1,0:T(8,128)(2,1)S(1)}, u32[]{:S(2)}, u32[]{:S(2)}) %all-to-all-start) | async-done | bytes 262176 | tf_op jit(solution)/shard_map/all_to_all | solution.py:181
  34.0 1.1 %covariances.1 = f32[256,128]{1,0:T(8,128)S(1)} custom-call(bf16[32,32,128]{2,1,0:T(8,128)(2,1)S(1)} %all-to-all-done.parts_ref, bf16[4,128,64]{2,1,0:T(8,128)(2,1)S(1)} %bitcast.15), custom_call_target="tpu_custom_call" | custom-call | tf_op jit(solution)/shard_map/covariances/pallas_call | solution.py:192
  35.1 15.7 %all_to_all.10 = f32[64,4,128]{2,1,0:T(4,128)S(1)} all-to-all(f32[64,4,128]{2,1,0:T(4,128)S(1)} %bitcast.16), channel_id=1, replica_groups={{336,344,320,328,368,376,352,360,272,280,256,264,304,312,288,296,464,47..., dimensions={0} | all-to-all | bytes 262144 | tf_op jit(solution)/shard_map/all_to_all | solution.py:205
  50.9 0.6 %maximum_multiply_fusion = f32[1,4,4,128]{3,2,1,0:T(4,128)} fusion(f32[1,1,4,128]{3,2,1,0:T(4,128)S(1)} %get-tuple-element.12, f32[1,1,4,128]{3,2,1,0:T(4,128)S(1)} %get-tuple-element.13, f32[1,1,4,128]{3,2,1,0:T(4,128)S(1)} %get-tuple-element.14, f32[1,1,4,128]{3,2,1,0:T(4,128)S(1)} %get-tuple-element.11), kind=kLoop, calls=%fused_computation.1 | loop fusion | flops 8192 | bytes 16384 | tf_op jit(solution)/shard_map/mul | solution.py:208
  (2 shorter events, 0.0 us)
Async XLA Ops:
  2.4 31.6 %all-to-all-start = ((bf16[32,32,128]{2,1,0:T(8,128)(2,1)}), bf16[32,32,128]{2,1,0:T(8,128)(2,1)S(1)}, u32[]{:S(2)}, u32[]{:S(2)}) async-start(bf16[32,32,128]{2,1,0:T(8,128)(2,1)} %transform.1), calls=%async_computation | async-start | bytes 524288 | tf_op jit(solution)/shard_map/all_to_all | solution.py:181
  21.4 0.7 %copy-start = (s32[32]{0:T(128)S(1)}, s32[32]{0:T(128)}, u32[]{:S(2)}) copy-start(s32[32]{0:T(128)} %param.10) | copy-start | bytes 388

commit v7 on v5

--- a/solution.py
+++ b/solution.py
@@ -108,23 +108,19 @@
                 one = jnp.concatenate([block[place_of[n][sub]][at] for n in range(sources)], axis=0)
                 n = (sub * lows + i + j) * lanes
                 by_order[n : n + lanes, :] = one.T
-    samples = 2 * highs * blocks
-    shape = (wide, 2 * samples)
-    same = (lax.broadcasted_iota(jnp.int32, shape, 0) < half) == (
-        lax.broadcasted_iota(jnp.int32, shape, 1) < samples
-    )
     for pair in range(pairs):
-        rows_of = [
-            by_order[pl.ds(high * width + 4 * pair + 2 * order + c, blocks, stride=lanes), :]
-            for order in range(2)
-            for high in range(highs)
-            for c in range(2)
-        ]
-        spectra = jnp.concatenate(rows_of, axis=0).astype(BF16)
-        coeffs = lax.dot_general(basis[pair], spectra, NT, preferred_element_type=F32)
-        coeffs = jnp.where(same, coeffs, 0.0).astype(BF16)
-        gram = lax.dot_general(coeffs, coeffs, NT, preferred_element_type=F32)
-        staged[pl.ds(pair, half, stride=pairs), :] = gram[:half] + gram[half:]
+        grams = []
+        for order in range(2):
+            rows_of = [
+                by_order[pl.ds(high * width + 4 * pair + 2 * order + c, blocks, stride=lanes), :]
+                for high in range(highs)
+                for c in range(2)
+            ]
+            spectra = jnp.concatenate(rows_of, axis=0).astype(BF16)
+            own = basis[pair, order * half : (order + 1) * half, :]
+            coeffs = lax.dot_general(own, spectra, NT, preferred_element_type=F32).astype(BF16)
+            grams.append(lax.dot_general(coeffs, coeffs, NT, preferred_element_type=F32))
+        staged[pl.ds(pair, half, stride=pairs), :] = jnp.concatenate(grams, axis=1)
     count = len(chunk_of) // 2
     step = out.shape[0] // count
     for here in range(count):

time: 51.2 us -> 51.9 us (1.014)
  Pallas kernels: 3.51 us -> 4.28 us
    pallas_call x1, Pallas kernels: 1.12 us -> 1.88 us  [local(): pl.pallas_call(functools.partial(covariances, place_of, img_order), out_s...]
where the time goes in v7:
time: 51.9 us; the launch traced here: 51.2 us
  starting transfers between devices  17.2 us (33%)
  blocking collectives  15.4 us (30%)
  waiting for transfers between devices  11.7 us (23%)
  Pallas kernels  4.28 us (8%)
  other arithmetic  1.64 us (3%)
  local copies, waits for them, and re-layouts  0.85 us (2%)
    all_to_all x1, starting transfers between devices, local(): lax.all_to_all(parts, ('img', 'bas'), 0, 0, tiled=True, axis_index_groups...  17.2 us
    all_to_all x1, blocking collectives, local(): lax.all_to_all(sent, 'img', 0, 0, tiled=True, axis_index_groups=[img_order])  15.4 us
    all_to_all x1, waiting for transfers between devices, local(): lax.all_to_all(parts, ('img', 'bas'), 0, 0, tiled=True, axis_index_groups...  11.7 us
    pallas_call x1, Pallas kernels, local(): pl.pallas_call(functools.partial(transform, sum(place_of, [])), out_shape...  2.39 us
    pallas_call x1, Pallas kernels, local(): pl.pallas_call(functools.partial(covariances, place_of, img_order), out_s...  1.88 us
  transfers between devices with their start and end apart: 1, of which 1 were waited for; matrix products, arithmetic and copies ran while one was open for 2% of the time, Pallas kernels for 0%

profile of v7, /device:TPU:6, one launch (start us, length us, event | category | flops | bytes accessed | tf_op | source)
XLA Modules:
  0.0 51.2 jit_solution(14101308105250573064)
XLA Ops:
  0.0 2.4 %transform.1 = bf16[32,32,128]{2,1,0:T(8,128)(2,1)} custom-call(s32[32]{0:T(128)} %groups_in.1, f32[64,64]{1,0:T(8,128)} %ctf_in.1, bf16[256,512]{1,0:T(8,128)(2,1)} %bitcast.18, bf16[2,64,8,256]{3,2,1,0:T(8,128)(2,1)} %constant.32.clone.table_in), custom_call_target="tpu_custom_call" | custom-call | tf_op jit(solution)/shard_map/transform/pallas_call | solution.py:151
  2.4 17.2 %all-to-all-start = ((bf16[32,32,128]{2,1,0:T(8,128)(2,1)}), bf16[32,32,128]{2,1,0:T(8,128)(2,1)S(1)}, u32[]{:S(2)}, u32[]{:S(2)}) async-start(bf16[32,32,128]{2,1,0:T(8,128)(2,1)} %transform.1), calls=%async_computation | async-start | bytes 524288 | tf_op jit(solution)/shard_map/all_to_all | solution.py:170
  19.6 0.0 copy-start
  19.6 0.6 %copy-done = s32[32]{0:T(128)S(1)} copy-done((s32[32]{0:T(128)S(1)}, s32[32]{0:T(128)}, u32[]{:S(2)}) %copy-start) | copy-done | bytes 152
  20.3 0.1 dynamic_slice.6
  20.4 0.1 iota_compare_fusion
  20.4 0.9 %select_bitcast_fusion = bf16[8,64,64]{1,2,0:T(8,128)(2,1)S(1)} fusion(bf16[32,64,64]{2,1,0:T(8,128)(2,1)} %param.9, s32[]{:T(128)S(6)} %select_n.16, pred[8,64]{1,0:T(8,128)(4,1)S(1)} %iota_compare_fusion), kind=kLoop, calls=%fused_computation | loop fusion | flops 32768 | bytes 131588 | tf_op jit(solution)/shard_map/transpose | solution.py:177
  21.4 0.1 copy.7
  21.5 11.7 %all-to-all-done.parts_ref = bf16[32,32,128]{2,1,0:T(8,128)(2,1)S(1)} async-done(((bf16[32,32,128]{2,1,0:T(8,128)(2,1)}), bf16[32,32,128]{2,1,0:T(8,128)(2,1)S(1)}, u32[]{:S(2)}, u32[]{:S(2)}) %all-to-all-start) | async-done | bytes 262176 | tf_op jit(solution)/shard_map/all_to_all | solution.py:170
  33.2 1.9 %covariances.1 = f32[256,128]{1,0:T(8,128)S(1)} custom-call(bf16[32,32,128]{2,1,0:T(8,128)(2,1)S(1)} %all-to-all-done.parts_ref, bf16[4,128,64]{2,1,0:T(8,128)(2,1)S(1)} %bitcast.15), custom_call_target="tpu_custom_call" | custom-call | tf_op jit(solution)/shard_map/covariances/pallas_call | solution.py:181
  35.1 15.4 %all_to_all.10 = f32[64,4,128]{2,1,0:T(4,128)S(1)} all-to-all(f32[64,4,128]{2,1,0:T(4,128)S(1)} %bitcast.16), channel_id=1, replica_groups={{336,344,320,328,368,376,352,360,272,280,256,264,304,312,288,296,464,47..., dimensions={0} | all-to-all | bytes 262144 | tf_op jit(solution)/shard_map/all_to_all | solution.py:194
  50.6 0.6 %maximum_multiply_fusion = f32[1,4,4,128]{3,2,1,0:T(4,128)} fusion(f32[1,1,4,128]{3,2,1,0:T(4,128)S(1)} %get-tuple-element.12, f32[1,1,4,128]{3,2,1,0:T(4,128)S(1)} %get-tuple-element.13, f32[1,1,4,128]{3,2,1,0:T(4,128)S(1)} %get-tuple-element.14, f32[1,1,4,128]{3,2,1,0:T(4,128)S(1)} %get-tuple-element.11), kind=kLoop, calls=%fused_computation.1 | loop fusion | flops 8192 | bytes 16384 | tf_op jit(solution)/shard_map/mul | solution.py:197
  (2 shorter events, 0.0 us)
Async XLA Ops:
  2.4 30.8 %all-to-all-start = ((bf16[32,32,128]{2,1,0:T(8,128)(2,1)}), bf16[32,32,128]{2,1,0:T(8,128)(2,1)S(1)}, u32[]{:S(2)}, u32[]{:S(2)}) async-start(bf16[32,32,128]{2,1,0:T(8,128)(2,1)} %transform.1), calls=%async_computation | async-start | bytes 524288 | tf_op jit(solution)/shard_map/all_to_all | solution.py:170
  19.6 0.7 %copy-start = (s32[32]{0:T(128)S(1)}, s32[32]{0:T(128)}, u32[]{:S(2)}) copy-start(s32[32]{0:T(128)} %param.10) | copy-start | bytes 388

commit v8 on v5

--- a/solution.py
+++ b/solution.py
@@ -144,7 +144,7 @@
     places = bas_size * pool
     shape = (places, lows * radii_dev, lanes)
     ring = [(high, sub, core) for high in range(bas_size // 2) for sub in range(pool) for core in range(2)]
-    start = 5 * places // 8
+    start = 11 * places // 16
     ring = ring[start:] + ring[:start]
     members = [(sub, 2 * high + core) for high, sub, core in ring]
     place_of = [[members.index((sub, bas)) for sub in range(pool)] for bas in range(bas_size)]

time: 51.2 us -> 51.2 us (level)
  starting transfers between devices: 17.2 us -> 16.3 us
  waiting for transfers between devices: 11.7 us -> 12.5 us
    all_to_all x1, starting transfers between devices: 17.2 us -> 16.3 us  [local(): lax.all_to_all(parts, ('img', 'bas'), 0, 0, tiled=True, axis_index_groups...]
    all_to_all x1, waiting for transfers between devices: 11.7 us -> 12.5 us  [local(): lax.all_to_all(parts, ('img', 'bas'), 0, 0, tiled=True, axis_index_groups...]
where the time goes in v8:
time: 51.2 us; the launch traced here: 50.4 us
  starting transfers between devices  16.3 us (32%)
  blocking collectives  15.5 us (30%)
  waiting for transfers between devices  12.5 us (24%)
  Pallas kernels  3.51 us (7%)
  other arithmetic  1.64 us (3%)
  local copies, waits for them, and re-layouts  0.85 us (2%)
    all_to_all x1, starting transfers between devices, local(): lax.all_to_all(parts, ('img', 'bas'), 0, 0, tiled=True, axis_index_groups...  16.3 us
    all_to_all x1, blocking collectives, local(): lax.all_to_all(sent, 'img', 0, 0, tiled=True, axis_index_groups=[img_order])  15.5 us
    all_to_all x1, waiting for transfers between devices, local(): lax.all_to_all(parts, ('img', 'bas'), 0, 0, tiled=True, axis_index_groups...  12.5 us
    pallas_call x1, Pallas kernels, local(): pl.pallas_call(functools.partial(transform, sum(place_of, [])), out_shape...  2.39 us
    pallas_call x1, Pallas kernels, local(): pl.pallas_call(functools.partial(covariances, place_of, img_order), out_s...  1.12 us
  transfers between devices with their start and end apart: 1, of which 1 were waited for; matrix products, arithmetic and copies ran while one was open for 2% of the time, Pallas kernels for 0%

profile of v8, /device:TPU:6, one launch (start us, length us, event | category | flops | bytes accessed | tf_op | source)
XLA Modules:
  0.0 50.4 jit_solution(3486173406144032238)
XLA Ops:
  0.0 2.4 %transform.1 = bf16[32,32,128]{2,1,0:T(8,128)(2,1)} custom-call(s32[32]{0:T(128)} %groups_in.1, f32[64,64]{1,0:T(8,128)} %ctf_in.1, bf16[256,512]{1,0:T(8,128)(2,1)} %bitcast.18, bf16[2,64,8,256]{3,2,1,0:T(8,128)(2,1)} %constant.32.clone.table_in), custom_call_target="tpu_custom_call" | custom-call | tf_op jit(solution)/shard_map/transform/pallas_call | solution.py:155
  2.4 16.3 %all-to-all-start = ((bf16[32,32,128]{2,1,0:T(8,128)(2,1)}), bf16[32,32,128]{2,1,0:T(8,128)(2,1)S(1)}, u32[]{:S(2)}, u32[]{:S(2)}) async-start(bf16[32,32,128]{2,1,0:T(8,128)(2,1)} %transform.1), calls=%async_computation | async-start | bytes 524288 | tf_op jit(solution)/shard_map/all_to_all | solution.py:174
  18.7 0.0 copy-start
  18.7 0.6 %copy-done = s32[32]{0:T(128)S(1)} copy-done((s32[32]{0:T(128)S(1)}, s32[32]{0:T(128)}, u32[]{:S(2)}) %copy-start) | copy-done | bytes 152
  19.4 0.1 dynamic_slice.6
  19.5 0.1 iota_compare_fusion
  19.5 0.9 %select_bitcast_fusion = bf16[8,64,64]{1,2,0:T(8,128)(2,1)S(1)} fusion(bf16[32,64,64]{2,1,0:T(8,128)(2,1)} %param.9, s32[]{:T(128)S(6)} %select_n.16, pred[8,64]{1,0:T(8,128)(4,1)S(1)} %iota_compare_fusion), kind=kLoop, calls=%fused_computation | loop fusion | flops 32768 | bytes 131588 | tf_op jit(solution)/shard_map/transpose | solution.py:181
  20.5 0.1 copy.7
  20.6 12.5 %all-to-all-done.parts_ref = bf16[32,32,128]{2,1,0:T(8,128)(2,1)S(1)} async-done(((bf16[32,32,128]{2,1,0:T(8,128)(2,1)}), bf16[32,32,128]{2,1,0:T(8,128)(2,1)S(1)}, u32[]{:S(2)}, u32[]{:S(2)}) %all-to-all-start) | async-done | bytes 262176 | tf_op jit(solution)/shard_map/all_to_all | solution.py:174
  33.1 1.1 %covariances.1 = f32[256,128]{1,0:T(8,128)S(1)} custom-call(bf16[32,32,128]{2,1,0:T(8,128)(2,1)S(1)} %all-to-all-done.parts_ref, bf16[4,128,64]{2,1,0:T(8,128)(2,1)S(1)} %bitcast.15), custom_call_target="tpu_custom_call" | custom-call | tf_op jit(solution)/shard_map/covariances/pallas_call | solution.py:185
  34.2 15.5 %all_to_all.10 = f32[64,4,128]{2,1,0:T(4,128)S(1)} all-to-all(f32[64,4,128]{2,1,0:T(4,128)S(1)} %bitcast.16), channel_id=1, replica_groups={{336,344,320,328,368,376,352,360,272,280,256,264,304,312,288,296,464,47..., dimensions={0} | all-to-all | bytes 262144 | tf_op jit(solution)/shard_map/all_to_all | solution.py:198
  49.8 0.6 %maximum_multiply_fusion = f32[1,4,4,128]{3,2,1,0:T(4,128)} fusion(f32[1,1,4,128]{3,2,1,0:T(4,128)S(1)} %get-tuple-element.12, f32[1,1,4,128]{3,2,1,0:T(4,128)S(1)} %get-tuple-element.13, f32[1,1,4,128]{3,2,1,0:T(4,128)S(1)} %get-tuple-element.14, f32[1,1,4,128]{3,2,1,0:T(4,128)S(1)} %get-tuple-element.11), kind=kLoop, calls=%fused_computation.1 | loop fusion | flops 8192 | bytes 16384 | tf_op jit(solution)/shard_map/mul | solution.py:201
  (2 shorter events, 0.0 us)
Async XLA Ops:
  2.4 30.7 %all-to-all-start = ((bf16[32,32,128]{2,1,0:T(8,128)(2,1)}), bf16[32,32,128]{2,1,0:T(8,128)(2,1)S(1)}, u32[]{:S(2)}, u32[]{:S(2)}) async-start(bf16[32,32,128]{2,1,0:T(8,128)(2,1)} %transform.1), calls=%async_computation | async-start | bytes 524288 | tf_op jit(solution)/shard_map/all_to_all | solution.py:174
  18.7 0.7 %copy-start = (s32[32]{0:T(128)S(1)}, s32[32]{0:T(128)}, u32[]{:S(2)}) copy-start(s32[32]{0:T(128)} %param.10) | copy-start | bytes 388
